TPU v7x, 32 devices: a whole 2x2x4 slice. The times are simulated.
32 devices in a mesh: dp: 8 (over z, core), fsdp: 4 (over y, x).
Axes of the slice: x: 2, y: 2, z: 4, core: 2. Of those that a mesh axis runs over, the one named last changes fastest.
Arguments:
- tokens: bfloat16 [32768, 768], P(('dp', 'fsdp')), may hold values from -6 to 6
- first_values: bfloat16 [32768, 384], P(('dp', 'fsdp')), may hold values from -6 to 6
- out_grad: bfloat16 [32768, 768], P(('dp', 'fsdp')), may hold values from -6 to 6
- lengths: int32 [32, 2], P(('dp', 'fsdp')), may hold values from 0 to 1024, as said below
- in_proj: bfloat16 [768, 1920], P(('dp', 'fsdp')), may hold values from -0.21875 to 0.21875
- out_proj: bfloat16 [768, 768], P(('dp', 'fsdp')), may hold values from -0.875 to 0.875
- up_proj: bfloat16 [768, 3072], P(('dp', 'fsdp')), may hold values from -0.21875 to 0.21875
- down_proj: bfloat16 [3072, 768], P(('dp', 'fsdp')), may hold values from -0.109375 to 0.109375
- vectors: bfloat16 [11, 768], P(None, ('dp', 'fsdp')), may hold values from -0.9 to 1.75, as said below
Outputs:
- output: float32 [32768, 768], P(('dp', 'fsdp'))
- input_grad: float32 [32768, 768], P(('dp', 'fsdp'))
- first_values_grad: float32 [32768, 384], P(('dp', 'fsdp'))
- in_proj_grad: float32 [768, 1920], P(('dp', 'fsdp'))
- out_proj_grad: float32 [768, 768], P(('dp', 'fsdp'))
- up_proj_grad: float32 [768, 3072], P(('dp', 'fsdp'))
- down_proj_grad: float32 [3072, 768], P(('dp', 'fsdp'))
- vectors_grad: float32 [11, 768], P(None, ('dp', 'fsdp'))
Inputs may be any that keep to these rules, and one draw needn't show every extreme that they name: `lengths`: each device holds either one sequence of 1024 tokens, given as (1024, 0), or two of half that length; both kinds occur in every draw. `vectors`: rows 0 and 4 are norm gains, the others shifts and biases.
All inputs are finite; a program needn't handle non-finite values.
Results may differ from a plain program's by a relative error of at most 0.0095.
Values may be sent and summed in bfloat16 or wider, within the bound.
No kernel may reach another device: no remote copies, remote signals or barrier semaphores. Data moves between devices by JAX's collectives and lax.ppermute only.
A program may use at most 256 MiB of HBM per device.

v0:
```python
import jax
import jax.numpy as jnp
from jax import lax
from jax.sharding import PartitionSpec as P

H = 12
HD = 64


EPS = 1e-05
NEG = -1000000000.0


def layer_norm(values, scale_row, shift_row):
    centred = values - jnp.mean(values, axis=-1, keepdims=True)
    spread = jnp.mean(centred * centred, axis=-1, keepdims=True)
    return centred * lax.rsqrt(spread + EPS) * scale_row + shift_row


def gelu_tanh(values):
    return jax.nn.gelu(values, approximate=True)


def over_rows(left_side, right_side):
    return lax.dot_general(
        left_side, right_side, (((0,), (0,)), ((), ())), preferred_element_type=jnp.float32
    )


def times_trans(left_side, right_side):
    return lax.dot_general(
        left_side, right_side, (((1,), (1,)), ((), ())), preferred_element_type=jnp.float32
    )


def body(tokens, first_values, out_grad, lengths, in_proj, out_proj, up_proj, down_proj, vectors):
    gathered = (
        lax.all_gather(in_proj, ("dp", "fsdp"), axis=0, tiled=True),
        lax.all_gather(out_proj, ("dp", "fsdp"), axis=0, tiled=True),
        lax.all_gather(up_proj, ("dp", "fsdp"), axis=0, tiled=True),
        lax.all_gather(down_proj, ("dp", "fsdp"), axis=0, tiled=True),
        lax.all_gather(vectors, ("dp", "fsdp"), axis=1, tiled=True),
    )
    full_in, full_out, full_up, full_down, full_vec = gathered
    vector_rows = full_vec.astype(jnp.float32)
    row_count = tokens.shape[0]
    model_width = tokens.shape[1]
    half_width = first_values.shape[1]
    scaling = HD ** (-0.5)
    tokens_f = tokens.astype(jnp.float32)
    normed, norm_one_back = jax.vjp(layer_norm, tokens_f, vector_rows[0], vector_rows[1])
    normed_bf = normed.astype(jnp.bfloat16)
    projected = jnp.dot(normed_bf, full_in, preferred_element_type=jnp.float32)
    queries = (projected[:, :model_width] + vector_rows[2]).astype(jnp.bfloat16)
    key_rows = projected[:, model_width : 2 * model_width].astype(jnp.bfloat16)
    fresh = projected[:, 2 * model_width :].astype(jnp.bfloat16)
    value_rows = jnp.concatenate([fresh, first_values], axis=1)
    query_heads = queries.reshape(row_count, H, HD)
    key_heads = key_rows.reshape(row_count, H, HD)
    value_heads = value_rows.reshape(row_count, H, HD)
    places = jnp.arange(row_count, dtype=jnp.int32)
    bounds = jnp.cumsum(lengths[0])
    segment = jnp.sum((places[:, None] >= bounds[None, :]).astype(jnp.int32), axis=1)
    block_rows = min(512, row_count)
    blocks = row_count // block_rows
    offsets = jnp.arange(blocks, dtype=jnp.int32) * block_rows

    def block_scores(offset):
        row_places = lax.dynamic_slice_in_dim(places, offset, block_rows, 0)
        row_segment = lax.dynamic_slice_in_dim(segment, offset, block_rows, 0)
        allowed = (row_segment[:, None] == segment[None, :]) & (
            row_places[:, None] >= places[None, :]
        )
        query_block = lax.dynamic_slice_in_dim(query_heads, offset, block_rows, 0)
        scores = (
            jnp.einsum("qhd,khd->hqk", query_block, key_heads, preferred_element_type=jnp.float32)
            * scaling
        )
        return (jnp.where(allowed[None], scores, NEG), query_block)

    def forward_block(offset):
        scores, query_block = block_scores(offset)
        row_peak = jnp.max(scores, axis=-1, keepdims=True)
        raised = jnp.exp(scores - row_peak)
        row_total = jnp.sum(raised, axis=-1, keepdims=True)
        attention = (raised / row_total).astype(jnp.bfloat16)
        context = jnp.einsum(
            "hqk,khd->qhd", attention, value_heads, preferred_element_type=jnp.float32
        )
        return (context, row_peak + jnp.log(row_total))

    contexts, log_totals = lax.map(forward_block, offsets)
    context = contexts.reshape(row_count, model_width).astype(jnp.bfloat16)
    branch = jnp.dot(context, full_out, preferred_element_type=jnp.float32) + vector_rows[3]
    middle = tokens_f + branch
    normed_two, norm_two_back = jax.vjp(layer_norm, middle, vector_rows[4], vector_rows[5])
    normed_two_bf = normed_two.astype(jnp.bfloat16)
    hidden = jnp.dot(normed_two_bf, full_up, preferred_element_type=jnp.float32) + vector_rows[
        7:
    ].reshape(-1)
    active, gelu_back = jax.vjp(gelu_tanh, hidden)
    active_bf = active.astype(jnp.bfloat16)
    output = (
        middle + jnp.dot(active_bf, full_down, preferred_element_type=jnp.float32) + vector_rows[6]
    )
    back_in, back_out, back_up, back_down = (
        lax.all_gather(in_proj, ("dp", "fsdp"), axis=0, tiled=True),
        lax.all_gather(out_proj, ("dp", "fsdp"), axis=0, tiled=True),
        lax.all_gather(up_proj, ("dp", "fsdp"), axis=0, tiled=True),
        lax.all_gather(down_proj, ("dp", "fsdp"), axis=0, tiled=True),
    )
    grad_rows = out_grad.astype(jnp.float32)
    grad_down = over_rows(active_bf, out_grad)
    bias_down = jnp.sum(grad_rows, axis=0)
    grad_active = times_trans(out_grad, back_down)
    grad_hidden = gelu_back(grad_active)[0].astype(jnp.bfloat16)
    grad_up = over_rows(normed_two_bf, grad_hidden)
    bias_up = jnp.sum(grad_hidden.astype(jnp.float32), axis=0)
    grad_normed_two = times_trans(grad_hidden, back_up)
    grad_middle, gain_two, shift_two = norm_two_back(grad_normed_two)
    grad_middle = grad_middle + grad_rows
    grad_branch = grad_middle.astype(jnp.bfloat16)
    grad_outp = over_rows(context, grad_branch)
    bias_out = jnp.sum(grad_branch.astype(jnp.float32), axis=0)
    grad_context = times_trans(grad_branch, back_out).astype(jnp.bfloat16).reshape(row_count, H, HD)

    def backward_block(running, packed):
        key_acc, value_acc = running
        offset, log_total = packed
        scores, query_block = block_scores(offset)
        attention = jnp.exp(scores - log_total)
        attention_bf = attention.astype(jnp.bfloat16)
        grad_block = lax.dynamic_slice_in_dim(grad_context, offset, block_rows, 0)
        grad_attention = jnp.einsum(
            "qhd,khd->hqk", grad_block, value_heads, preferred_element_type=jnp.float32
        )
        weighted = jnp.sum(attention * grad_attention, axis=-1, keepdims=True)
        grad_scores = (attention * (grad_attention - weighted)).astype(jnp.bfloat16)
        grad_query = (
            jnp.einsum("hqk,khd->qhd", grad_scores, key_heads, preferred_element_type=jnp.float32)
            * scaling
        )
        key_acc = (
            key_acc
            + jnp.einsum(
                "hqk,qhd->khd", grad_scores, query_block, preferred_element_type=jnp.float32
            )
            * scaling
        )
        value_acc = value_acc + jnp.einsum(
            "hqk,qhd->khd", attention_bf, grad_block, preferred_element_type=jnp.float32
        )
        return ((key_acc, value_acc), grad_query)

    empty_acc = jnp.zeros((row_count, H, HD), jnp.float32)
    sums_kv, grad_queries = lax.scan(backward_block, (empty_acc, empty_acc), (offsets, log_totals))
    grad_keys, grad_values = sums_kv
    grad_queries = grad_queries.reshape(row_count, model_width).astype(jnp.bfloat16)
    grad_keys = grad_keys.reshape(row_count, model_width).astype(jnp.bfloat16)
    grad_values = grad_values.reshape(row_count, model_width)
    grad_fresh = grad_values[:, :half_width].astype(jnp.bfloat16)
    first_grad = grad_values[:, half_width:]
    grad_proj = jnp.concatenate([grad_queries, grad_keys, grad_fresh], axis=1)
    grad_in = over_rows(normed_bf, grad_proj)
    bias_query = jnp.sum(grad_queries.astype(jnp.float32), axis=0)
    grad_normed = times_trans(grad_proj, back_in)
    grad_tokens, gain_one, shift_one = norm_one_back(grad_normed)
    input_grad = grad_tokens + grad_middle
    grad_vec = jnp.concatenate(
        [
            jnp.stack([gain_one, shift_one, bias_query, bias_out, gain_two, shift_two, bias_down]),
            bias_up.reshape(-1, model_width),
        ],
        axis=0,
    )
    shards = (
        lax.psum_scatter(grad_in, ("dp", "fsdp"), scatter_dimension=0, tiled=True),
        lax.psum_scatter(grad_outp, ("dp", "fsdp"), scatter_dimension=0, tiled=True),
        lax.psum_scatter(grad_up, ("dp", "fsdp"), scatter_dimension=0, tiled=True),
        lax.psum_scatter(grad_down, ("dp", "fsdp"), scatter_dimension=0, tiled=True),
        lax.psum_scatter(grad_vec, ("dp", "fsdp"), scatter_dimension=1, tiled=True),
    )
    return (output, input_grad, first_grad, shards[0], shards[1], shards[2], shards[3], shards[4])


def solution(mesh):
    placed = (
        P(("dp", "fsdp"), None),
        P(("dp", "fsdp"), None),
        P(("dp", "fsdp"), None),
        P(("dp", "fsdp"), None),
        P(("dp", "fsdp"), None),
        P(("dp", "fsdp"), None),
        P(("dp", "fsdp"), None),
        P(("dp", "fsdp"), None),
        P(None, ("dp", "fsdp")),
    )
    return jax.shard_map(
        body,
        mesh=mesh,
        in_specs=placed,
        out_specs=(
            P(("dp", "fsdp"), None),
            P(("dp", "fsdp"), None),
            P(("dp", "fsdp"), None),
            P(("dp", "fsdp"), None),
            P(("dp", "fsdp"), None),
            P(("dp", "fsdp"), None),
            P(("dp", "fsdp"), None),
            P(None, ("dp", "fsdp")),
        ),
        check_vma=False,
    )
```

profile of v0, /device:TPU:0, one launch (start us, length us, event | category | flops | bytes accessed | tf_op | source)
XLA Modules:
  0.0 899.0 jit_solution(1110848041910054295)
XLA Ops:
  10.0 70.9 %all-gather = bf16[32,24,11]{1,2,0:T(8,128)(2,1)S(1)} all-gather(bf16[1,24,11]{1,2,0:T(8,128)(2,1)} %bitcast.111), channel_id=1, replica_groups=mesh['dp'=8,'fsdp'=4] {'dp','fsdp'}, dimensions={0}, use_global_device_ids=true | all-gather | bytes 17424 | tf_op jit(solution)/shard_map/all_gather | solution.py:42
  104.9 76.3 %while.29 = (s32[]{:T(128)}, bf16[2,512,12,64]{1,3,2,0:T(8,128)(2,1)}, f32[2,12,512,1]{2,1,3,0:T(8,128)S(1)}, s32[2]{0:T(128)S(1)}, s32[1024]{0:T(1024)S(1)}, /*...) while((s32[]{:T(128)}, ...), condition=%wide.region_7.8_spmd.clone, body=%wide.region_4.7_spmd.clone.sunk | while | flops 1687676928 | bytes 190296304 | solution.py:92
  108.2 10.9 %fusion.106 = (f32[12,512]{1,0:T(8,128)S(1)}, f32[12,512,1024]{2,1,0:T(8,128)}) fusion(pred[512,1024]{1,0:T(8,128)(4,1)S(1)} %compare_and_fusion.4, bf16[1024,12,64]{0,2,1:T(8,128)(2,1)S(1)} %get-tuple-element.521, bf16[1024,12,64]{0,2,1:T(8,128)(2,1)S(1)} %get-tuple-element.520, s32[]{:T(128)S(6)} %select_n.57), kind=kOutput, calls=%fused_computation.3.clone.1 | convolution fusion | flops 824174592 | bytes 28073988 | tf_op jit(solution)/shard_map/while/body/eval_jaxpr/qhd,khd->hqk/dot_general | solution.py:76
  119.1 12.4 %fusion.107 = f32[12,512]{1,0:T(8,128)S(1)} fusion(f32[12,512,1024]{2,1,0:T(8,128)} %get-tuple-element.474, f32[12,512]{1,0:T(8,128)S(1)} %get-tuple-element.475, pred[512,1024]{1,0:T(8,128)(4,1)S(1)} %compare_and_fusion.4), kind=kLoop, calls=%fused_computation.4.clone.1 | loop fusion | flops 25159680 | bytes 25739264 | tf_op jit(solution)/shard_map/while/body/eval_jaxpr/reduce_sum | solution.py:85
  146.4 10.9 %fusion.106 = (f32[12,512]{1,0:T(8,128)S(1)}, f32[12,512,1024]{2,1,0:T(8,128)}) fusion(pred[512,1024]{1,0:T(8,128)(4,1)S(1)} %compare_and_fusion.4, bf16[1024,12,64]{0,2,1:T(8,128)(2,1)S(1)} %get-tuple-element.521, bf16[1024,12,64]{0,2,1:T(8,128)(2,1)S(1)} %get-tuple-element.520, s32[]{:T(128)S(6)} %select_n.57), kind=kOutput, calls=%fused_computation.3.clone.1 | convolution fusion | flops 824174592 | bytes 28073988 | tf_op jit(solution)/shard_map/while/body/eval_jaxpr/qhd,khd->hqk/dot_general | solution.py:76
  157.2 12.3 %fusion.107 = f32[12,512]{1,0:T(8,128)S(1)} fusion(f32[12,512,1024]{2,1,0:T(8,128)} %get-tuple-element.474, f32[12,512]{1,0:T(8,128)S(1)} %get-tuple-element.475, pred[512,1024]{1,0:T(8,128)(4,1)S(1)} %compare_and_fusion.4), kind=kLoop, calls=%fused_computation.4.clone.1 | loop fusion | flops 25159680 | bytes 25739264 | tf_op jit(solution)/shard_map/while/body/eval_jaxpr/reduce_sum | solution.py:85
  193.9 11.5 %fusion.58 = f32[1024,3072]{1,0:T(8,128)} fusion(bf16[768,3072]{1,0:T(8,128)(2,1)} %all-gather.10.cloned.1.call-done, f32[1024,768]{0,1:T(8,128)} %copy-done.6, f32[768]{0:T(1024)S(1)} %copy-done.31, f32[768]{0:T(1024)S(1)} %copy-done.27, f32[1024]{0:T(1024)S(1)} %fusion.51, f32[1024]{0:T(1024)S(1)} %broadcast_multiply_fusion), kind=kOutput, calls=%fused_computation.109 | convolution fusion | flops 4835770368 | bytes 20461568 | tf_op jit(solution)/shard_map/dot_general | solution.py:98
  205.3 53.7 %all-gather.12.cloned.1.call-done = bf16[3072,768]{1,0:T(8,128)(2,1)} async-done(((bf16[96,768]{1,0:T(8,128)(2,1)}), bf16[3072,768]{1,0:T(8,128)(2,1)}) %all-gather.12.cloned.1.call-update) | async-done | bytes 4718608 | tf_op jit(solution)/shard_map/all_gather | solution.py:41
  259.0 16.9 %convert_reduce_fusion = (f32[3072]{0:T(1024)}, bf16[1024,3072]{1,0:T(8,128)(2,1)S(1)}) fusion(f32[1024,3072]{1,0:T(8,128)} %fusion.58, f32[3072]{0:T(1024)S(1)} %copy-done.45, bf16[1024,768]{1,0:T(8,128)(2,1)} %param.15, bf16[3072,768]{1,0:T(8,128)(2,1)} %all-gather.12.cloned.1.call-done), kind=kOutput, calls=%fused_computation.46 | convolution fusion | flops 4904186880 | bytes 25190400 | tf_op jit(solution)/shard_map/dot_general | solution.py:31
  303.8 178.9 %while.30 = (s32[]{:T(128)}, f32[1024,12,64]{0,2,1:T(8,128)}, f32[1024,12,64]{0,2,1:T(8,128)}, bf16[2,512,12,64]{1,3,2,0:T(8,128)(2,1)}, s32[2]{0:T(128)S(1)}, /...) while((s32[]{:T(128)}, f32[1024,12,64]{0,2,1:T(8,128)}, ...), condition=%wide.region_14.15_spmd.clone.clone, body=%wide.region_12.14_spmd.clone.clone.sunk | while | flops 4126795776 | bytes 231936336 | solution.py:156
  307.3 13.4 %fusion.117 = f32[12,512,1024]{2,1,0:T(8,128)} fusion(bf16[1024,12,64]{0,2,1:T(8,128)(2,1)S(1)} %get-tuple-element.564, bf16[1024,12,64]{0,2,1:T(8,128)(2,1)} %copy-done.1, s32[]{:T(128)S(6)} %select_n.61), kind=kOutput, calls=%fused_computation.28.clone.1 | convolution fusion | flops 805306368 | bytes 27525124 | tf_op jit(solution)/shard_map/while/body/eval_jaxpr/qhd,khd->hqk/dot_general | solution.py:76
  320.7 13.8 %bitcast_add_fusion.5 = f32[1024,12,64]{0,2,1:T(8,128)} fusion(f32[1024,12,64]{0,2,1:T(8,128)} %get-tuple-element.543, f32[12,512,1024]{2,1,0:T(8,128)} %fusion.117, f32[12,512]{1,0:T(8,128)S(1)} %dynamic-slice_bitcast_fusion.2, pred[512,1024]{1,0:T(8,128)(4,1)S(1)} %compare_and_fusion.5, pred[]{:T(512)S(6)} %compare.3, ...), kind=kOutput, calls=%fused_computation.20.clone.1 | convolution fusion | flops 832045056 | bytes 32800772 | tf_op jit(solution)/shard_map/while/body/eval_jaxpr/hqk,qhd->khd/dot_general | solution.py:150
  334.5 18.2 %multiply_reduce_fusion.5 = (f32[12,512]{1,0:T(8,128)S(1)}, f32[12,512,1024]{2,1,0:T(8,128)}) fusion(f32[12,512,1024]{2,1,0:T(8,128)} %fusion.117, f32[12,512]{1,0:T(8,128)S(1)} %dynamic-slice_bitcast_fusion.2, pred[512,1024]{1,0:T(8,128)(4,1)S(1)} %compare_and_fusion.5, bf16[1024,12,64]{0,2,1:T(8,128)(2,1)} %get-tuple-element.567, ...), kind=kOutput, calls=%fused_computation.15.clone.1 | convolution fusion | flops 836757504 | bytes 53264388 | tf_op jit(solution)/shard_map/while/body/eval_jaxpr/qhd,khd->hqk/dot_general | solution.py:134
  352.7 22.1 %multiply_convert_fusion.5 = bf16[12,512,1024]{2,1,0:T(8,128)(2,1)} fusion(f32[12,512,1024]{2,1,0:T(8,128)} %get-tuple-element.488, f32[12,512,1024]{2,1,0:T(8,128)} %fusion.117, f32[12,512]{1,0:T(8,128)S(1)} %get-tuple-element.489, f32[12,512]{1,0:T(8,128)S(1)} %dynamic-slice_bitcast_fusion.2, pred[512,1024]{1,0:T(8,128)(4,1)S(1)} %compare_and_fusion.5), kind=kLoop, calls=%fused_computation.14.clone.1 | loop fusion | flops 37748736 | bytes 63488000 | tf_op jit(solution)/shard_map/while/body/eval_jaxpr/convert_element_type | solution.py:138
  396.3 13.2 %fusion.117 = f32[12,512,1024]{2,1,0:T(8,128)} fusion(bf16[1024,12,64]{0,2,1:T(8,128)(2,1)S(1)} %get-tuple-element.564, bf16[1024,12,64]{0,2,1:T(8,128)(2,1)} %copy-done.1, s32[]{:T(128)S(6)} %select_n.61), kind=kOutput, calls=%fused_computation.28.clone.1 | convolution fusion | flops 805306368 | bytes 27525124 | tf_op jit(solution)/shard_map/while/body/eval_jaxpr/qhd,khd->hqk/dot_general | solution.py:76
  409.5 14.5 %bitcast_add_fusion.5 = f32[1024,12,64]{0,2,1:T(8,128)} fusion(f32[1024,12,64]{0,2,1:T(8,128)} %get-tuple-element.543, f32[12,512,1024]{2,1,0:T(8,128)} %fusion.117, f32[12,512]{1,0:T(8,128)S(1)} %dynamic-slice_bitcast_fusion.2, pred[512,1024]{1,0:T(8,128)(4,1)S(1)} %compare_and_fusion.5, pred[]{:T(512)S(6)} %compare.3, ...), kind=kOutput, calls=%fused_computation.20.clone.1 | convolution fusion | flops 832045056 | bytes 32800772 | tf_op jit(solution)/shard_map/while/body/eval_jaxpr/hqk,qhd->khd/dot_general | solution.py:150
  424.1 18.2 %multiply_reduce_fusion.5 = (f32[12,512]{1,0:T(8,128)S(1)}, f32[12,512,1024]{2,1,0:T(8,128)}) fusion(f32[12,512,1024]{2,1,0:T(8,128)} %fusion.117, f32[12,512]{1,0:T(8,128)S(1)} %dynamic-slice_bitcast_fusion.2, pred[512,1024]{1,0:T(8,128)(4,1)S(1)} %compare_and_fusion.5, bf16[1024,12,64]{0,2,1:T(8,128)(2,1)} %get-tuple-element.567, ...), kind=kOutput, calls=%fused_computation.15.clone.1 | convolution fusion | flops 836757504 | bytes 53264388 | tf_op jit(solution)/shard_map/while/body/eval_jaxpr/qhd,khd->hqk/dot_general | solution.py:134
  442.3 21.2 %multiply_convert_fusion.5 = bf16[12,512,1024]{2,1,0:T(8,128)(2,1)} fusion(f32[12,512,1024]{2,1,0:T(8,128)} %get-tuple-element.488, f32[12,512,1024]{2,1,0:T(8,128)} %fusion.117, f32[12,512]{1,0:T(8,128)S(1)} %get-tuple-element.489, f32[12,512]{1,0:T(8,128)S(1)} %dynamic-slice_bitcast_fusion.2, pred[512,1024]{1,0:T(8,128)(4,1)S(1)} %compare_and_fusion.5), kind=kLoop, calls=%fused_computation.14.clone.1 | loop fusion | flops 37748736 | bytes 63488000 | tf_op jit(solution)/shard_map/while/body/eval_jaxpr/convert_element_type | solution.py:138
  497.0 13.3 %fusion.59 = f32[3072,768]{1,0:T(8,128)} fusion(bf16[1024,768]{1,0:T(8,128)(2,1)} %param.15, f32[1024,3072]{1,0:T(8,128)} %fusion.58, f32[3072]{0:T(1024)S(1)} %copy-done.46), kind=kOutput, calls=%fused_computation.110 | convolution fusion | flops 4863295488 | bytes 23605248 | tf_op jit(solution)/shard_map/dot_general | solution.py:25
  511.1 11.1 %fusion.57 = f32[768,3072]{1,0:T(8,128)} fusion(bf16[1024,3072]{1,0:T(8,128)(2,1)} %copy-done.53, f32[1024,768]{0,1:T(8,128)} %copy-done.6, f32[768]{0:T(1024)S(1)} %copy-done.32, f32[768]{0:T(1024)S(1)} %copy-done.28, f32[1024]{0:T(1024)S(1)} %copy-done.30, f32[1024]{0:T(1024)S(1)} %copy-done.26), kind=kOutput, calls=%fused_computation.108 | convolution fusion | flops 4835770368 | bytes 18888704 | tf_op jit(solution)/shard_map/dot_general | solution.py:25
  525.2 12.3 %add_add_fusion.3 = f32[1024,768]{0,1:T(8,128)} fusion(f32[1024,768]{0,1:T(8,128)S(1)} %copy-done.8, bf16[3072,768]{1,0:T(8,128)(2,1)} %all-gather.12.cloned.1.call-done, f32[768]{0:T(1024)S(1)} %copy-done.48, f32[1024,3072]{1,0:T(8,128)} %fusion.58, f32[3072]{0:T(1024)S(1)} %copy-done.46), kind=kOutput, calls=%fused_computation.74 | convolution fusion | flops 4864868352 | bytes 23608320 | tf_op jit(solution)/shard_map/dot_general | solution.py:104
  569.0 40.2 %all-reduce.1 = f32[11,768]{1,0:T(8,128)S(1)} all-reduce(f32[11,768]{1,0:T(8,128)S(1)} %concatenate.11), channel_id=6, replica_groups=mesh['dp'=8,'fsdp'=4] {'dp','fsdp'}, use_global_device_ids=true, to_apply=%region_29.30.clone | all-reduce | flops 8448 | bytes 67584
  610.0 141.0 %reduce-scatter.12.cloned.1.call-done = f32[96,768]{1,0:T(8,128)} async-done(((f32[3072,768]{1,0:T(8,128)}), f32[96,768]{1,0:T(8,128)}) %reduce-scatter.12.cloned.1.call-update) | async-done | bytes 294928 | tf_op jit(solution)/shard_map/reduce_scatter | solution.py:180
  750.9 141.1 %reduce-scatter.10.cloned.1.call-done = f32[24,3072]{1,0:T(8,128)} async-done(((f32[768,3072]{1,0:T(8,128)}), f32[24,3072]{1,0:T(8,128)}) %reduce-scatter.10.cloned.1.call-update) | async-done | bytes 294928 | tf_op jit(solution)/shard_map/reduce_scatter | solution.py:179
  (237 shorter events, 182.5 us)
Async XLA Ops:
  7.2 80.6 %all-gather.6.cloned.1.call-start = ((), (), s32[]{:S(2)}) async-start(), calls=%async_computation.4 | async-start | bytes 3041280 | tf_op jit(solution)/shard_map/all_gather | solution.py:38
  7.9 178.0 %all-gather.8.cloned.1.call-start = ((), (), s32[]{:S(2)}) async-start(), calls=%async_computation.5 | async-start | bytes 1216512 | tf_op jit(solution)/shard_map/all_gather | solution.py:39
  8.6 185.2 %all-gather.10.cloned.1.call-start = ((), (), s32[]{:S(2)}) async-start(), calls=%async_computation.6 | async-start | bytes 4866048 | tf_op jit(solution)/shard_map/all_gather | solution.py:40
  9.4 249.6 %all-gather.12.cloned.1.call-start = ((), (), s32[]{:S(2)}) async-start(), calls=%async_computation.7 | async-start | bytes 4866048 | tf_op jit(solution)/shard_map/all_gather | solution.py:41
  10.0 600.0 %reduce-scatter.8.cloned.1.call-start = ((), (), s32[]{:S(2)}) async-start(), calls=%async_computation.8 | async-start | bytes 2433024 | tf_op jit(solution)/shard_map/reduce_scatter | solution.py:178
  85.6 7.7 copy-start.33
  86.1 7.3 copy-start.41
  86.1 7.3 copy-start.37
  108.2 23.3 %copy-start.3 = (bf16[1024,12,64]{0,2,1:T(8,128)(2,1)S(1)}, bf16[1024,12,64]{0,2,1:T(8,128)(2,1)}, u32[]{:S(2)}) copy-start(bf16[1024,12,64]{0,2,1:T(8,128)(2,1)} %get-tuple-element.522) | copy-start | bytes 4718596 | tf_op jit(solution)/shard_map/while
  119.1 15.5 %copy-start = (f32[12,512,1024]{2,1,0:T(8,128)S(1)}, f32[12,512,1024]{2,1,0:T(8,128)}, u32[]{:S(2)}) copy-start(f32[12,512,1024]{2,1,0:T(8,128)} %get-tuple-element.474) | copy-start | bytes 75497472 | tf_op jit(solution)/shard_map/while
  146.4 23.2 %copy-start.3 = (bf16[1024,12,64]{0,2,1:T(8,128)(2,1)S(1)}, bf16[1024,12,64]{0,2,1:T(8,128)(2,1)}, u32[]{:S(2)}) copy-start(bf16[1024,12,64]{0,2,1:T(8,128)(2,1)} %get-tuple-element.522) | copy-start | bytes 4718596 | tf_op jit(solution)/shard_map/while
  157.2 15.5 %copy-start = (f32[12,512,1024]{2,1,0:T(8,128)S(1)}, f32[12,512,1024]{2,1,0:T(8,128)}, u32[]{:S(2)}) copy-start(f32[12,512,1024]{2,1,0:T(8,128)} %get-tuple-element.474) | copy-start | bytes 75497472 | tf_op jit(solution)/shard_map/while
  189.8 101.6 %copy-start.25 = (f32[1024]{0:T(1024)}, f32[1024]{0:T(1024)S(1)}, u32[]{:S(2)}) copy-start(f32[1024]{0:T(1024)S(1)} %broadcast_multiply_fusion) | copy-start | bytes 12292
  191.9 99.6 %copy-start.29 = (f32[1024]{0:T(1024)}, f32[1024]{0:T(1024)S(1)}, u32[]{:S(2)}) copy-start(f32[1024]{0:T(1024)S(1)} %fusion.51) | copy-start | bytes 12292
  193.9 65.1 %copy-start.45 = (f32[3072]{0:T(1024)S(1)}, f32[3072]{0:T(1024)}, u32[]{:S(2)}) copy-start(f32[3072]{0:T(1024)} %add.162) | copy-start | bytes 36868
  259.0 17.0 %copy-start.17 = (bf16[768,3072]{1,0:T(8,128)(2,1)S(1)}, bf16[768,3072]{1,0:T(8,128)(2,1)}, u32[]{:S(2)}) copy-start(bf16[768,3072]{1,0:T(8,128)(2,1)} %all-gather.10.cloned.1.call-done) | copy-start | bytes 14155780
  276.0 7.3 copy-start.53
  298.1 311.8 %reduce-scatter.14.cloned.1.call-start = ((), (), s32[]{:S(2)}) async-start(), calls=%async_computation.11 | async-start | bytes 6082560
  307.3 13.5 %copy-start.16 = (bf16[1024,12,64]{0,2,1:T(8,128)(2,1)S(1)}, bf16[1024,12,64]{0,2,1:T(8,128)(2,1)}, u32[]{:S(2)}) copy-start(bf16[1024,12,64]{0,2,1:T(8,128)(2,1)} %get-tuple-element.566) | copy-start | bytes 4718596 | tf_op jit(solution)/shard_map/while
  374.9 9.6 %copy-start.2 = (bf16[1024,12,64]{0,2,1:T(8,128)(2,1)S(1)}, bf16[1024,12,64]{0,2,1:T(8,128)(2,1)}, u32[]{:S(2)}) copy-start(bf16[1024,12,64]{0,2,1:T(8,128)(2,1)} %copy-done.1) | copy-start | bytes 4718596 | tf_op jit(solution)/shard_map/while
  396.3 13.2 %copy-start.16 = (bf16[1024,12,64]{0,2,1:T(8,128)(2,1)S(1)}, bf16[1024,12,64]{0,2,1:T(8,128)(2,1)}, u32[]{:S(2)}) copy-start(bf16[1024,12,64]{0,2,1:T(8,128)(2,1)} %get-tuple-element.566) | copy-start | bytes 4718596 | tf_op jit(solution)/shard_map/while
  463.5 9.5 %copy-start.2 = (bf16[1024,12,64]{0,2,1:T(8,128)(2,1)S(1)}, bf16[1024,12,64]{0,2,1:T(8,128)(2,1)}, u32[]{:S(2)}) copy-start(bf16[1024,12,64]{0,2,1:T(8,128)(2,1)} %copy-done.1) | copy-start | bytes 4718596 | tf_op jit(solution)/shard_map/while
  496.4 254.6 %reduce-scatter.12.cloned.1.call-start = ((), (), s32[]{:S(2)}) async-start(), calls=%async_computation.10 | async-start | bytes 9732096 | tf_op jit(solution)/shard_map/reduce_scatter | solution.py:180
  510.4 381.6 %reduce-scatter.10.cloned.1.call-start = ((), (), s32[]{:S(2)}) async-start(), calls=%async_computation.9 | async-start | bytes 9732096 | tf_op jit(solution)/shard_map/reduce_scatter | solution.py:179
  (43 other events, 121.0 us)
Sparse Core Ops, SparseCore 0:
  10.9 61.5 all-gather.5
  75.4 52.9 all-gather.7
  131.3 62.5 all-gather.9
  196.6 62.3 all-gather.11
  298.3 97.8 reduce-scatter.7
  496.5 112.0 reduce-scatter.13
  616.1 134.8 reduce-scatter.11
  757.4 134.5 reduce-scatter.9
where the time goes:
time: 906 us; the launch traced here: 899 us
  waiting for transfers between devices  340 us (38%)
  matrix products  271 us (30%)
  blocking collectives  111 us (12%)
  other arithmetic  91.2 us (10%)
  local copies, waits for them, and re-layouts  61.7 us (7%)
  between operations  14.9 us (2%)
    reduce_scatter x1, waiting for transfers between devices, body(): lax.psum_scatter(grad_up, ('dp', 'fsdp'), scatter_dimension=0, tiled=True)  141 us
    reduce_scatter x1, waiting for transfers between devices, body(): lax.psum_scatter(grad_down, ('dp', 'fsdp'), scatter_dimension=0, tiled=True)  141 us
    all_gather x1, blocking collectives, body(): lax.all_gather(vectors, ('dp', 'fsdp'), axis=1, tiled=True)  70.9 us
    all_gather x1, waiting for transfers between devices, body(): lax.all_gather(down_proj, ('dp', 'fsdp'), axis=0, tiled=True)  53.7 us
    dot_general x4, matrix products, block_scores(): jnp.einsum('qhd,khd->hqk', query_block, key_heads, preferred_element_type...  48.4 us
    convert_element_type x2, other arithmetic, backward_block(): grad_scores = (attention * (grad_attention - weighted)).astype(jnp.bfloat16)  43.3 us
    unnamed x1, blocking collectives  40.2 us
    dot_general x4, matrix products, times_trans(): lax.dot_general(left_side, right_side, (((1,), (1,)), ((), ())), preferre...  37 us
  transfers between devices with their start and end apart: 8, of which 4 were waited for; matrix products, arithmetic and copies ran while one was open for 42% of the time, Pallas kernels for 0%

commit v1 on v0

v1 whole, which is shorter than its diff:
```python
import functools

import jax
import jax.numpy as jnp
import numpy as np
from jax import lax
from jax.experimental import pallas as pl
from jax.experimental.pallas import tpu as pltpu
from jax.sharding import PartitionSpec as P

H = 12
HD = 64
EPS = 1e-05
NEG = -1000000000.0
LANES = 128
AXES = ("dp", "fsdp")
BF = jnp.bfloat16
F32 = jnp.float32
VMEM_LIMIT = 56 * 1024 * 1024
GELU_C = 0.7978845608028654
GELU_A = 0.044715


def dot(a, b):
    return lax.dot_general(a, b, (((1,), (0,)), ((), ())), preferred_element_type=F32)


def dot_rt(a, b):
    return lax.dot_general(a, b, (((1,), (1,)), ((), ())), preferred_element_type=F32)


def dot_lt(a, b):
    return lax.dot_general(a, b, (((0,), (0,)), ((), ())), preferred_element_type=F32)


def params(grid_rank=1):
    return pltpu.CompilerParams(
        vmem_limit_bytes=VMEM_LIMIT, dimension_semantics=("arbitrary",) * grid_rank
    )


def cost(flops, nbytes, trans=0):
    return pl.CostEstimate(flops=int(flops), bytes_accessed=int(nbytes), transcendentals=int(trans))


def norm_parts(values):
    centred = values - jnp.mean(values, axis=-1, keepdims=True)
    spread = jnp.mean(centred * centred, axis=-1, keepdims=True)
    rs = lax.rsqrt(spread + EPS)
    return centred * rs, rs


def norm_back(normed, rs, gain, grad):
    scaled = grad * gain
    m1 = jnp.mean(scaled, axis=-1, keepdims=True)
    m2 = jnp.mean(scaled * normed, axis=-1, keepdims=True)
    return rs * (scaled - m1 - normed * m2)


def in_kernel(x_ref, fv_ref, w_ref, a1_ref, qkv_ref, vec_ref):
    width = x_ref.shape[1]
    cols = w_ref.shape[1] - LANES

    @pl.when(pl.program_id(0) == 0)
    def _():
        turned = jnp.transpose(w_ref[:, cols:].astype(F32))
        vec_ref[...] = turned[: vec_ref.shape[0]]

    normed, _ = norm_parts(x_ref[...].astype(F32))
    a1 = (normed * vec_ref[0:1, :] + vec_ref[1:2, :]).astype(BF)
    a1_ref[...] = a1
    proj = dot(a1, w_ref[:, :cols])
    queries = (proj[:, :width] + vec_ref[2:3, :]).astype(BF)
    qkv_ref[:, :width] = queries * jnp.asarray(HD**-0.5, BF)
    qkv_ref[:, width:cols] = proj[:, width:].astype(BF)
    qkv_ref[:, cols:] = fv_ref[...]


def in_forward(tokens, first_values, w_in):
    rows, width = tokens.shape
    half = first_values.shape[1]
    cols = w_in.shape[1] - LANES
    block = 256
    return pl.pallas_call(
        in_kernel,
        grid=(rows // block,),
        in_specs=[
            pl.BlockSpec((block, width), lambda i: (i, 0)),
            pl.BlockSpec((block, half), lambda i: (i, 0)),
            pl.BlockSpec(w_in.shape, lambda i: (0, 0)),
        ],
        out_specs=[
            pl.BlockSpec((block, width), lambda i: (i, 0)),
            pl.BlockSpec((block, cols + half), lambda i: (i, 0)),
            pl.BlockSpec((16, width), lambda i: (0, 0)),
        ],
        out_shape=[
            jax.ShapeDtypeStruct((rows, width), BF),
            jax.ShapeDtypeStruct((rows, cols + half), BF),
            jax.ShapeDtypeStruct((16, width), F32),
        ],
        compiler_params=params(),
        cost_estimate=cost(2 * rows * width * cols, 12e6),
        name="in_forward",
    )(tokens, first_values, w_in)


def lanes_of(shape):
    return lax.broadcasted_iota(jnp.int32, shape, 1)


def own_lanes(e, shape):
    lane = lanes_of(shape)
    return (lane < HD) if e == 0 else (lane >= HD)


def spare(e):
    return HD if e == 0 else 0


def split3(values):
    hi = values.astype(BF).astype(F32)
    rest = values - hi
    mid = rest.astype(BF).astype(F32)
    return hi, mid, rest - mid


def attn_fwd_kernel(bound_ref, q_ref, k_ref, v_ref, ctx_ref, qa_ref):
    rows = q_ref.shape[0]
    block = 256
    bound = bound_ref[0, 0]
    shape = (block, LANES)
    lane = lanes_of(shape)
    place = lax.broadcasted_iota(jnp.int32, (rows, LANES), 0)
    all_lane = lanes_of((rows, LANES))
    k_all = k_ref[...]
    values = jnp.concatenate([v_ref[...], jnp.ones((rows, LANES), BF)], axis=1)
    tri = lax.broadcasted_iota(jnp.int32, (block, block), 0) >= lax.broadcasted_iota(
        jnp.int32, (block, block), 1
    )
    ctxs = [[None, None] for _ in range(rows // block)]
    for e in range(2):
        sp = spare(e)
        k_aux = jnp.where((all_lane == sp) & (place < bound), 1.0, 0.0).astype(BF)
        k_aug = jnp.where(own_lanes(e, (rows, LANES)), k_all, k_aux)
        for j in range(rows // block):
            lo, hi = j * block, (j + 1) * block
            seg = lax.broadcasted_iota(jnp.int32, shape, 0) + lo >= bound
            q_aux = jnp.where((lane == sp) & seg, NEG, 0.0)
            own = own_lanes(e, shape)
            q_aug = jnp.where(own, q_ref[lo:hi, :].astype(F32), q_aux)
            s = dot_rt(q_aug.astype(BF), k_aug[:hi, :])
            s_diag = jnp.where(tri, s[:, lo:], NEG)
            s = s_diag if j == 0 else jnp.concatenate([s[:, :lo], s_diag], axis=1)
            peak = jnp.max(s, axis=-1, keepdims=True)
            p = jnp.exp(s - peak).astype(BF)
            o = dot(p, values[:hi, :])
            total = o[:, LANES:]
            ctxs[j][e] = o[:, :LANES] / total
            l_hi, l_mid, l_lo = split3(-(peak + jnp.log(total)))
            q_aug = jnp.where(
                lane == sp + 1,
                l_hi,
                jnp.where(lane == sp + 2, l_mid, jnp.where(lane == sp + 3, l_lo, q_aug)),
            )
            qa_ref[lo:hi, e * LANES : (e + 1) * LANES] = q_aug.astype(BF)
    for j in range(rows // block):
        ctx_ref[j * block : (j + 1) * block, :] = jnp.where(
            lane < HD, ctxs[j][0], ctxs[j][1]
        ).astype(BF)


def attn_forward(lengths, qkv, width):
    rows = qkv.shape[0]
    pairs = width // LANES
    slab = lambda off: pl.BlockSpec((rows, LANES), lambda j, off=off: (0, off + j))
    return pl.pallas_call(
        attn_fwd_kernel,
        grid=(pairs,),
        in_specs=[
            pl.BlockSpec(memory_space=pltpu.SMEM),
            slab(0),
            slab(pairs),
            slab(2 * pairs),
        ],
        out_specs=[slab(0), pl.BlockSpec((rows, 2 * LANES), lambda j: (0, j))],
        out_shape=[
            jax.ShapeDtypeStruct((rows, width), BF),
            jax.ShapeDtypeStruct((rows, 2 * width), BF),
        ],
        compiler_params=params(),
        cost_estimate=cost(2 * 2 * rows * rows * 256 * H * 0.63, 9e6, rows * rows * H),
        name="attn_forward",
    )(lengths, qkv, qkv, qkv)


def attn_bwd_kernel(
    bound_ref, qa_ref, k_ref, v_ref, ctx_ref, do_ref, dq_ref, dk_ref, dv_ref, fv_ref, dk_acc, dv_acc
):
    rows = k_ref.shape[0]
    block = 256
    bound = bound_ref[0, 0]
    full = (rows, LANES)
    lane = lanes_of(full)
    place = lax.broadcasted_iota(jnp.int32, full, 0)
    k_all = k_ref[...].astype(F32)
    v_all = v_ref[...].astype(F32)
    do_all = do_ref[...].astype(F32)
    prod = do_all * ctx_ref[...].astype(F32)
    tri = lax.broadcasted_iota(jnp.int32, (block, block), 0) <= lax.broadcasted_iota(
        jnp.int32, (block, block), 1
    )
    dqs = [[None, None] for _ in range(rows // block)]
    for e in range(2):
        sp = spare(e)
        own = own_lanes(e, full)
        three = (lane >= sp + 1) & (lane <= sp + 3)
        k_aux = jnp.where(three | ((lane == sp) & (place < bound)), 1.0, 0.0)
        k_aug = jnp.where(own, k_all, k_aux).astype(BF)
        v_aug = jnp.where(own, v_all, jnp.where(three, 1.0, 0.0)).astype(BF)
        delta = jnp.sum(jnp.where(own, prod, 0.0), axis=-1, keepdims=True)
        d_hi, d_mid, d_lo = split3(-delta)
        do_aug = jnp.where(
            own,
            do_all,
            jnp.where(
                lane == sp + 1,
                d_hi,
                jnp.where(lane == sp + 2, d_mid, jnp.where(lane == sp + 3, d_lo, 0.0)),
            ),
        ).astype(BF)
        qa = qa_ref[:, e * LANES : (e + 1) * LANES]
        for j in reversed(range(rows // block)):
            lo, hi = j * block, (j + 1) * block
            qa_j = qa[lo:hi, :]
            do_j = do_aug[lo:hi, :]
            s = dot_rt(k_aug[:hi, :], qa_j)
            s_diag = jnp.where(tri, s[lo:, :], NEG)
            s = s_diag if j == 0 else jnp.concatenate([s[:lo, :], s_diag], axis=0)
            p = jnp.exp(s)
            ds = (p * dot_rt(v_aug[:hi, :], do_j)).astype(BF)
            dv_j = dot(p.astype(BF), do_j)
            dk_j = dot(ds, qa_j)
            if j == rows // block - 1:
                dv_acc[e] = dv_j
                dk_acc[e] = dk_j
            else:
                dv_acc[e, :hi, :] += dv_j
                dk_acc[e, :hi, :] += dk_j
            dqs[j][e] = dot_lt(ds, k_aug[:hi, :])
    for j in range(rows // block):
        sel = lanes_of((block, LANES)) < HD
        dq_ref[j * block : (j + 1) * block, :] = (
            jnp.where(sel, dqs[j][0], dqs[j][1]) * HD**-0.5
        ).astype(BF)
    dk_ref[...] = jnp.where(lane < HD, dk_acc[0], dk_acc[1]).astype(BF)
    dv = jnp.where(lane < HD, dv_acc[0], dv_acc[1])
    fresh = pl.num_programs(0) // 2

    @pl.when(pl.program_id(0) < fresh)
    def _():
        dv_ref[...] = dv.astype(BF)

    @pl.when(pl.program_id(0) >= fresh)
    def _():
        fv_ref[...] = dv


def attn_backward(lengths, qa, qkv, ctx, dctx):
    rows, width = ctx.shape
    pairs = width // LANES
    fresh = pairs // 2
    slab = lambda off: pl.BlockSpec((rows, LANES), lambda j, off=off: (0, off + j))
    return pl.pallas_call(
        attn_bwd_kernel,
        grid=(pairs,),
        in_specs=[
            pl.BlockSpec(memory_space=pltpu.SMEM),
            pl.BlockSpec((rows, 2 * LANES), lambda j: (0, j)),
            slab(pairs),
            slab(2 * pairs),
            slab(0),
            slab(0),
        ],
        out_specs=[
            slab(0),
            slab(0),
            pl.BlockSpec((rows, LANES), lambda j: (0, jnp.minimum(j, fresh - 1))),
            pl.BlockSpec((rows, LANES), lambda j: (0, jnp.maximum(j - fresh, 0))),
        ],
        out_shape=[
            jax.ShapeDtypeStruct((rows, width), BF),
            jax.ShapeDtypeStruct((rows, width), BF),
            jax.ShapeDtypeStruct((rows, width // 2), BF),
            jax.ShapeDtypeStruct((rows, width // 2), F32),
        ],
        scratch_shapes=[
            pltpu.VMEM((2, rows, LANES), F32),
            pltpu.VMEM((2, rows, LANES), F32),
        ],
        compiler_params=params(),
        cost_estimate=cost(5 * 2 * rows * rows * 256 * H * 0.63, 15e6, rows * rows * H),
        name="attn_backward",
    )(lengths, qa, qkv, qkv, ctx, dctx)


def ffn_kernel(ctx_ref, x_ref, wo_ref, wu_ref, vec_ref, mid_ref, a2_ref, act_ref, gd_ref):
    width = x_ref.shape[1]
    branch = dot(ctx_ref[...], wo_ref[...]) + vec_ref[3:4, :]
    mid = x_ref[...].astype(F32) + branch
    mid_ref[...] = mid
    normed, _ = norm_parts(mid)
    a2 = (normed * vec_ref[4:5, :] + vec_ref[5:6, :]).astype(BF)
    a2_ref[...] = a2
    for g in range(wu_ref.shape[1] // width):
        part = slice(g * width, (g + 1) * width)
        u = dot(a2, wu_ref[:, part]) + vec_ref[7 + g : 8 + g, :]
        u2 = u * u
        t = jnp.tanh(u * (GELU_C + (GELU_C * GELU_A) * u2))
        act = u * (0.5 + 0.5 * t)
        act_ref[:, part] = act.astype(BF)
        slope = (0.5 + 0.5 * t) + act * (1.0 - t) * (GELU_C + (3.0 * GELU_C * GELU_A) * u2)
        gd_ref[:, part] = slope.astype(BF)


def ffn_forward(ctx, tokens, w_out, w_up, vec):
    rows, width = tokens.shape
    hidden = w_up.shape[1]
    block = 256
    by_rows = lambda n: pl.BlockSpec((block, n), lambda i: (i, 0))
    whole = lambda a: pl.BlockSpec(a.shape, lambda i: (0, 0))
    return pl.pallas_call(
        ffn_kernel,
        grid=(rows // block,),
        in_specs=[by_rows(width), by_rows(width), whole(w_out), whole(w_up), whole(vec)],
        out_specs=[by_rows(width), by_rows(width), by_rows(hidden), by_rows(hidden)],
        out_shape=[
            jax.ShapeDtypeStruct((rows, width), F32),
            jax.ShapeDtypeStruct((rows, width), BF),
            jax.ShapeDtypeStruct((rows, hidden), BF),
            jax.ShapeDtypeStruct((rows, hidden), BF),
        ],
        compiler_params=params(),
        cost_estimate=cost(2 * rows * width * (width + hidden), 28e6, rows * hidden),
        name="ffn_forward",
    )(ctx, tokens, w_out, w_up, vec)


def out_kernel(act_ref, mid_ref, wd_ref, vec_ref, out_ref):
    out_ref[...] = mid_ref[...] + dot(act_ref[...], wd_ref[...]) + vec_ref[6:7, :]


def out_forward(act, mid, w_down, vec):
    rows, width = mid.shape
    hidden = act.shape[1]
    block = 256
    by_rows = lambda n: pl.BlockSpec((block, n), lambda i: (i, 0))
    whole = lambda a: pl.BlockSpec(a.shape, lambda i: (0, 0))
    return pl.pallas_call(
        out_kernel,
        grid=(rows // block,),
        in_specs=[by_rows(hidden), by_rows(width), whole(w_down), whole(vec)],
        out_specs=by_rows(width),
        out_shape=jax.ShapeDtypeStruct((rows, width), F32),
        compiler_params=params(),
        cost_estimate=cost(2 * rows * width * hidden, 18e6),
        name="out_forward",
    )(act, mid, w_down, vec)


def store_units(table_ref, result, keep_ref, send_ref, units, first, core_bit, put):
    half = keep_ref.shape[0]
    size = result.shape[0] // units
    for mine in range(2):

        @pl.when(table_ref[half * 2] == mine)
        def _(mine=mine):
            for i in range(units):
                d = first + i
                place = table_ref[d]
                rows = result[i * size : (i + 1) * size, :].astype(BF)
                if ((d >> core_bit) & 1) == mine:
                    put(keep_ref, place, rows)
                else:
                    put(send_ref, place - half, rows)


def put_rows(ref, place, rows):
    ref[place] = rows


def down_grad_kernel(table_ref, act_ref, dy_ref, keep_ref, send_ref, *, core_bit):
    half, size, _ = keep_ref.shape
    units = act_ref.shape[1] // size
    result = dot_lt(act_ref[...], dy_ref[...])
    g = pl.program_id(0)
    mine = table_ref[2 * half]
    for i in range(units):
        d = g * units + i
        place = table_ref[d]
        rows = result[i * size : (i + 1) * size, :].astype(BF)
        core = lax.rem(lax.shift_right_logical(d, core_bit), 2)

        @pl.when(core == mine)
        def _():
            keep_ref[place] = rows

        @pl.when(core != mine)
        def _():
            send_ref[place - half] = rows


def down_grad(table, act, dy, n, core_bit):
    rows, hidden = act.shape
    width = dy.shape[1]
    unit = hidden // n
    block = 384
    whole = pl.BlockSpec((n // 2, unit, width), lambda g: (0, 0, 0))
    shape = jax.ShapeDtypeStruct((n // 2, unit, width), BF)
    return pl.pallas_call(
        functools.partial(down_grad_kernel, core_bit=core_bit),
        grid=(hidden // block,),
        in_specs=[
            pl.BlockSpec(memory_space=pltpu.SMEM),
            pl.BlockSpec((rows, block), lambda g: (0, g)),
            pl.BlockSpec((rows, width), lambda g: (0, 0)),
        ],
        out_specs=[whole, whole],
        out_shape=[shape, shape],
        compiler_params=params(),
        cost_estimate=cost(2 * rows * width * hidden, 13e6),
        name="down_grad",
    )(table, act, dy)


def up_grad_kernel(
    table_ref, dy_ref, wd_ref, gd_ref, a2_ref, du_ref, sums_ref, keep_ref, send_ref, a2t, *, core_bit
):
    @pl.when(pl.program_id(0) == 0)
    def _():
        a2t[...] = jnp.transpose(a2_ref[...])

    du = (dot_rt(dy_ref[...], wd_ref[...]) * gd_ref[...].astype(F32)).astype(BF)
    du_ref[...] = du
    sums_ref[...] = jnp.sum(du.astype(F32), axis=0, keepdims=True)
    result = dot(a2t[...], du)
    n = keep_ref.shape[0] * 2
    store_units(table_ref, result, keep_ref, send_ref, n, 0, core_bit, put_rows)


def up_grad(table, dy, w_down, gd, a2, n, core_bit):
    rows, width = dy.shape
    hidden = w_down.shape[0]
    unit = width // n
    block = 512
    part = pl.BlockSpec((n // 2, unit, block), lambda g: (0, 0, g))
    shape = jax.ShapeDtypeStruct((n // 2, unit, hidden), BF)
    whole = lambda a: pl.BlockSpec(a.shape, lambda g: (0, 0))
    return pl.pallas_call(
        functools.partial(up_grad_kernel, core_bit=core_bit),
        grid=(hidden // block,),
        in_specs=[
            pl.BlockSpec(memory_space=pltpu.SMEM),
            whole(dy),
            pl.BlockSpec((block, width), lambda g: (g, 0)),
            pl.BlockSpec((rows, block), lambda g: (0, g)),
            whole(a2),
        ],
        out_specs=[
            pl.BlockSpec((rows, block), lambda g: (0, g)),
            pl.BlockSpec((1, block), lambda g: (0, g)),
            part,
            part,
        ],
        out_shape=[
            jax.ShapeDtypeStruct((rows, hidden), BF),
            jax.ShapeDtypeStruct((1, hidden), F32),
            shape,
            shape,
        ],
        scratch_shapes=[pltpu.VMEM((width, rows), BF)],
        compiler_params=params(),
        cost_estimate=cost(4 * rows * width * hidden, 25e6),
        name="up_grad",
    )(table, dy, w_down, gd, a2)


def mid_back_kernel(
    table_ref,
    du_ref,
    wu_ref,
    mid_ref,
    dy_ref,
    ctx_ref,
    wo_ref,
    vec_ref,
    dmid_ref,
    dctx_ref,
    sums_ref,
    keep_ref,
    send_ref,
    acc,
    *,
    core_bit,
):
    i = pl.program_id(0)
    da2 = dot_rt(du_ref[...], wu_ref[...])
    normed, rs = norm_parts(mid_ref[...])
    dy = dy_ref[...].astype(F32)
    dmid = norm_back(normed, rs, vec_ref[4:5, :], da2) + dy
    dmid_ref[...] = dmid
    dbr = dmid.astype(BF)
    dctx_ref[...] = dot_rt(dbr, wo_ref[...]).astype(BF)
    total = lambda v: jnp.sum(v, axis=0, keepdims=True)
    sums = jnp.concatenate(
        [
            total(dbr.astype(F32)),
            total(da2 * normed),
            total(da2),
            total(dy),
            jnp.zeros((4, dy.shape[1]), F32),
        ],
        axis=0,
    )
    part = dot_lt(ctx_ref[...], dbr)

    @pl.when(i == 0)
    def _():
        sums_ref[...] = sums
        acc[...] = part

    @pl.when(i > 0)
    def _():
        sums_ref[...] += sums
        acc[...] += part

    @pl.when(i == pl.num_programs(0) - 1)
    def _():
        n = keep_ref.shape[0] * 2
        store_units(table_ref, acc, keep_ref, send_ref, n, 0, core_bit, put_rows)


def mid_back(table, du, w_up, mid, dy, ctx, w_out, vec, n, core_bit):
    rows, width = dy.shape
    hidden = du.shape[1]
    unit = width // n
    block = 256
    by_rows = lambda m: pl.BlockSpec((block, m), lambda i: (i, 0))
    whole = lambda a: pl.BlockSpec(a.shape, lambda i: (0, 0))
    units = pl.BlockSpec((n // 2, unit, width), lambda i: (0, 0, 0))
    shape = jax.ShapeDtypeStruct((n // 2, unit, width), BF)
    return pl.pallas_call(
        functools.partial(mid_back_kernel, core_bit=core_bit),
        grid=(rows // block,),
        in_specs=[
            pl.BlockSpec(memory_space=pltpu.SMEM),
            by_rows(hidden),
            whole(w_up),
            by_rows(width),
            by_rows(width),
            by_rows(width),
            whole(w_out),
            whole(vec),
        ],
        out_specs=[
            by_rows(width),
            by_rows(width),
            pl.BlockSpec((8, width), lambda i: (0, 0)),
            units,
            units,
        ],
        out_shape=[
            jax.ShapeDtypeStruct((rows, width), F32),
            jax.ShapeDtypeStruct((rows, width), BF),
            jax.ShapeDtypeStruct((8, width), F32),
            shape,
            shape,
        ],
        scratch_shapes=[pltpu.VMEM((width, width), F32)],
        compiler_params=params(),
        cost_estimate=cost(2 * rows * width * (hidden + 2 * width), 26e6),
        name="mid_back",
    )(table, du, w_up, mid, dy, ctx, w_out, vec)


def token_grad_kernel(
    x_ref, dq_ref, dk_ref, dv_ref, w_ref, dmid_ref, vec_ref, grad_ref, sums_ref
):
    width = x_ref.shape[1]
    i = pl.program_id(0)
    dq = dq_ref[...]
    dproj = jnp.concatenate([dq, dk_ref[...], dv_ref[...]], axis=1)
    da1 = dot_rt(dproj, w_ref[:, : dproj.shape[1]])
    normed, rs = norm_parts(x_ref[...].astype(F32))
    grad_ref[...] = dmid_ref[...] + norm_back(normed, rs, vec_ref[0:1, :], da1)
    total = lambda v: jnp.sum(v, axis=0, keepdims=True)
    sums = jnp.concatenate(
        [total(da1 * normed), total(da1), total(dq.astype(F32)), jnp.zeros((5, width), F32)], axis=0
    )

    @pl.when(i == 0)
    def _():
        sums_ref[...] = sums

    @pl.when(i > 0)
    def _():
        sums_ref[...] += sums


def token_grad(tokens, dq, dk, dfresh, w_in, dmid, vec):
    rows, width = tokens.shape
    half = dfresh.shape[1]
    block = 256
    by_rows = lambda m: pl.BlockSpec((block, m), lambda i: (i, 0))
    whole = lambda a: pl.BlockSpec(a.shape, lambda i: (0, 0))
    return pl.pallas_call(
        token_grad_kernel,
        grid=(rows // block,),
        in_specs=[
            by_rows(width),
            by_rows(width),
            by_rows(width),
            by_rows(half),
            whole(w_in),
            by_rows(width),
            whole(vec),
        ],
        out_specs=[by_rows(width), pl.BlockSpec((8, width), lambda i: (0, 0))],
        out_shape=[
            jax.ShapeDtypeStruct((rows, width), F32),
            jax.ShapeDtypeStruct((8, width), F32),
        ],
        compiler_params=params(),
        cost_estimate=cost(2 * rows * width * (2 * width + half), 17e6),
        name="token_grad",
    )(tokens, dq, dk, dfresh, w_in, dmid, vec)


def in_grad_kernel(
    table_ref, a1_ref, dq_ref, dk_ref, dv_ref, s1_ref, s2_ref, c1_ref, keep_ref, send_ref, *, core_bit
):
    width = a1_ref.shape[1]
    n = keep_ref.shape[0] * 2
    a1t = jnp.transpose(a1_ref[...])
    start = 0
    for ref in (dq_ref, dk_ref, dv_ref):
        for c in range(0, ref.shape[1], 384):
            result = dot(a1t, ref[:, c : c + 384])

            def put(out, place, rows, at=start):
                out[place, :, at : at + rows.shape[1]] = rows

            store_units(table_ref, result, keep_ref, send_ref, n, 0, core_bit, put)
            start += 384
    stacked = jnp.concatenate(
        [s1_ref[0:3, :], s2_ref[0:4, :]]
        + [c1_ref[0:1, g * width : (g + 1) * width] for g in range(c1_ref.shape[1] // width)]
        + [jnp.zeros((LANES - 7 - c1_ref.shape[1] // width, width), F32)],
        axis=0,
    )

    def put_last(out, place, rows):
        out[place, :, start:] = rows

    store_units(
        table_ref, jnp.transpose(stacked), keep_ref, send_ref, n, 0, core_bit, put_last
    )


def in_grad(table, a1, dq, dk, dfresh, s1, s2, c1, n, core_bit):
    rows, width = a1.shape
    cols = 2 * width + dfresh.shape[1]
    shape = jax.ShapeDtypeStruct((n // 2, width // n, cols + LANES), BF)
    vmem = pl.BlockSpec(memory_space=pltpu.VMEM)
    return pl.pallas_call(
        functools.partial(in_grad_kernel, core_bit=core_bit),
        in_specs=[pl.BlockSpec(memory_space=pltpu.SMEM)] + [vmem] * 7,
        out_specs=[vmem, vmem],
        out_shape=[shape, shape],
        compiler_params=pltpu.CompilerParams(vmem_limit_bytes=VMEM_LIMIT),
        cost_estimate=cost(2 * rows * width * cols, 12e6),
        name="in_grad",
    )(table, a1, dq, dk, dfresh, s1, s2, c1)


def stages_of(n_dp, n_fsdp):
    fsdp_bits = n_fsdp.bit_length() - 1
    dp_bits = n_dp.bit_length() - 1
    low = list(range(fsdp_bits // 2))[::-1]
    high = list(range(fsdp_bits // 2, fsdp_bits))[::-1]
    z_bits = list(range(fsdp_bits + 1, fsdp_bits + dp_bits))[::-1]
    core = fsdp_bits
    return core, ([core] + high + low + z_bits, [core] + low + high + z_bits)


def place_table(n_dp, n_fsdp):
    core, orders = stages_of(n_dp, n_fsdp)
    n = n_dp * n_fsdp
    table = np.zeros((n, n + 1), np.int32)
    for me in range(n):
        for d in range(n):
            order = orders[(d >> core) & 1]
            away = d ^ me
            place = 0
            for bit in order:
                place = place * 2 + ((away >> bit) & 1)
            table[me, d] = place
        table[me, n] = (me >> core) & 1
    return table


def swap(value, n_dp, n_fsdp, stage):
    core, orders = stages_of(n_dp, n_fsdp)
    pairs = [(i, i ^ (1 << orders[(i >> core) & 1][stage])) for i in range(n_dp * n_fsdp)]
    return lax.ppermute(value, AXES, pairs)


def reduce_units(keep, send, n_dp, n_fsdp):
    count = (n_dp * n_fsdp).bit_length() - 1
    for stage in range(count):
        got = swap(send, n_dp, n_fsdp, stage)
        total = keep.astype(F32) + got.astype(F32)
        if stage == count - 1:
            return total[0]
        half = total.shape[0] // 2
        keep = total[:half].astype(BF)
        send = total[half:].astype(BF)


def body(tokens, first_values, out_grad, lengths, in_proj, out_proj, up_proj, down_proj, vectors, *, n_dp, n_fsdp):
    n = n_dp * n_fsdp
    width = tokens.shape[1]
    hidden = up_proj.shape[1]
    vrows = vectors.shape[0]
    core_bit, _ = stages_of(n_dp, n_fsdp)
    me = lax.axis_index("dp") * n_fsdp + lax.axis_index("fsdp")
    table = lax.dynamic_slice(jnp.asarray(place_table(n_dp, n_fsdp)), (me, 0), (1, n + 1))[0]

    vec_t = jnp.pad(vectors.T, ((0, 0), (0, LANES - vrows)))
    gather = lambda a: lax.all_gather(a, AXES, axis=0, tiled=True)
    w_in = gather(jnp.concatenate([in_proj, vec_t], axis=1))
    w_out = gather(out_proj)
    w_up = gather(up_proj)
    w_down = gather(down_proj)

    a1, qkv, vec = in_forward(tokens, first_values, w_in)
    ctx, qa = attn_forward(lengths, qkv, width)
    mid, a2, act, gd = ffn_forward(ctx, tokens, w_out, w_up, vec)

    reduce = functools.partial(reduce_units, n_dp=n_dp, n_fsdp=n_fsdp)
    g_down = reduce(*down_grad(table, act, out_grad, n, core_bit))
    output = out_forward(act, mid, w_down, vec)
    du, dc1, keep, send = up_grad(table, out_grad, w_down, gd, a2, n, core_bit)
    g_up = reduce(keep, send)
    dmid, dctx, sums2, keep, send = mid_back(
        table, du, w_up, mid, out_grad, ctx, w_out, vec, n, core_bit
    )
    g_out = reduce(keep, send)
    dq, dk, dfresh, first_grad = attn_backward(lengths, qa, qkv, ctx, dctx)
    input_grad, sums1 = token_grad(tokens, dq, dk, dfresh, w_in, dmid, vec)
    g_in = reduce(*in_grad(table, a1, dq, dk, dfresh, sums1, sums2, dc1, n, core_bit))
    cols = in_proj.shape[1]
    g_vec = g_in[:, cols : cols + vrows].T
    return (output, input_grad, first_grad, g_in[:, :cols], g_out, g_up, g_down, g_vec)


def solution(mesh):
    rows = P(AXES, None)
    cols = P(None, AXES)
    return jax.shard_map(
        functools.partial(body, n_dp=mesh.shape["dp"], n_fsdp=mesh.shape["fsdp"]),
        mesh=mesh,
        in_specs=(rows,) * 8 + (cols,),
        out_specs=(rows,) * 7 + (cols,),
        check_vma=False,
    )
```

time: 906 us -> 461 us (0.51)
  matrix products: 271 us -> 0 us
  Pallas kernels: 0 us -> 153 us
  blocking collectives: 111 us -> 0 us
  waiting for transfers between devices: 340 us -> 257 us
  other arithmetic: 91.2 us -> 9.38 us
  local copies, waits for them, and re-layouts: 61.7 us -> 3.83 us
  starting transfers between devices: 0.31 us -> 22.5 us
    reduce_scatter x3 -> x0, waiting for transfers between devices: 282 us -> none  [the longest x1 141 us: body(): lax.psum_scatter(grad_up, ('dp', 'fsdp'), scatter_dimension=0, tiled=True)]
    dot_general x26 -> x0, matrix products: 271 us -> none  [the longest x4 48.4 us: block_scores(): jnp.einsum('qhd,khd->hqk', query_block, key_heads, preferred_element_type...]
    pallas_call x0 -> x10, Pallas kernels: none -> 153 us  [the longest x1 27.8 us: attn_backward(): pl.pallas_call(attn_bwd_kernel, grid=(pairs,), in_specs=[pl.BlockSpec(mem...]
    all_gather x4, waiting for transfers between devices: 55.7 us -> 199 us  [body(): gather = lambda a: lax.all_gather(a, AXES, axis=0, tiled=True)]
    all_gather x1 -> x0, blocking collectives: 70.9 us -> none  [body(): lax.all_gather(vectors, ('dp', 'fsdp'), axis=1, tiled=True)]
    ppermute x0 -> x20, waiting for transfers between devices: none -> 56.6 us  [swap(): return lax.ppermute(value, AXES, pairs)]
    convert_element_type x4 -> x0, other arithmetic: 45.8 us -> none  [the longest x2 43.3 us: backward_block(): grad_scores = (attention * (grad_attention - weighted)).astype(jnp.bfloat16)]
    unnamed x1 -> x0, blocking collectives: 40.2 us -> none
  transfers between devices with their start and end apart: 8 -> 24, of which waited for: 4 -> 14; matrix products, arithmetic and copies ran while one was open for 42% -> 2% of each run, Pallas kernels for 0% -> 26%
where the time goes in v1:
time: 461 us; the launch traced here: 460 us
  waiting for transfers between devices  257 us (56%)
  Pallas kernels  153 us (33%)
  starting transfers between devices  22.5 us (5%)
  between operations  14.1 us (3%)
  other arithmetic  9.38 us (2%)
    all_gather x4, waiting for transfers between devices, body(): gather = lambda a: lax.all_gather(a, AXES, axis=0, tiled=True)  199 us
    ppermute x20, waiting for transfers between devices, swap(): return lax.ppermute(value, AXES, pairs)  56.6 us
    pallas_call x1, Pallas kernels, attn_backward(): pl.pallas_call(attn_bwd_kernel, grid=(pairs,), in_specs=[pl.BlockSpec(mem...  27.8 us
    ppermute x20, starting transfers between devices, swap(): return lax.ppermute(value, AXES, pairs)  22.3 us
    pallas_call x1, Pallas kernels, attn_forward(): pl.pallas_call(attn_fwd_kernel, grid=(pairs,), in_specs=[pl.BlockSpec(mem...  21.1 us
    pallas_call x1, Pallas kernels, mid_back(): pl.pallas_call(functools.partial(mid_back_kernel, core_bit=core_bit), gri...  19.2 us
    pallas_call x1, Pallas kernels, ffn_forward(): pl.pallas_call(ffn_kernel, grid=(rows // block,), in_specs=[by_rows(width...  18.5 us
    pallas_call x1, Pallas kernels, up_grad(): pl.pallas_call(functools.partial(up_grad_kernel, core_bit=core_bit), grid...  16.6 us
  transfers between devices with their start and end apart: 24, of which 14 were waited for; matrix products, arithmetic and copies ran while one was open for 2% of the time, Pallas kernels for 26%

profile of v1, /device:TPU:0, one launch (start us, length us, event | category | flops | bytes accessed | tf_op | source)
XLA Modules:
  0.0 460.3 jit_solution(5599445708485352447)
XLA Ops:
  12.8 60.4 %all-gather.5.cloned.1.call-done.w_ref = bf16[768,2048]{1,0:T(8,128)(2,1)} async-done(((bf16[24,2048]{1,0:T(8,128)(2,1)}), bf16[768,2048]{1,0:T(8,128)(2,1)}) %all-gather.5.cloned.1.call-update) | async-done | bytes 3145744 | tf_op jit(solution)/shard_map/all_gather | solution.py:740
  73.3 8.6 %in_forward.1 = (bf16[1024,768]{1,0:T(8,128)(2,1)}, bf16[1024,2304]{1,0:T(8,128)(2,1)}, f32[16,768]{1,0:T(8,128)}) custom-call(bf16[1024,768]{1,0:T(8,128)(2,1)} %x_ref.5, bf16[1024,384]{1,0:T(8,128)(2,1)} %fv_ref.1, bf16[768,2048]{1,0:T(8,128)(2,1)} %all-gather.5.cloned.1.call-done.w_ref), custom_call_target="tpu_custom_call" | custom-call | flops 3019898880 | bytes 12000000 | tf_op jit(solution)/shard_map/in_forward/pallas_call | solution.py:84
  81.8 21.1 %attn_forward.1 = (bf16[1024,768]{1,0:T(8,128)(2,1)}, bf16[1024,1536]{1,0:T(8,128)(2,1)}) custom-call(s32[1,2]{1,0:T(1,128)} %bound_ref.3, bf16[1024,2304]{1,0:T(8,128)(2,1)} %get-tuple-element.36.q_ref.k_ref.v_ref, bf16[1024,2304]{1,0:T(8,128)(2,1)} %get-tuple-element.36.q_ref.k_ref.v_ref, bf16[1024,2304]{1,0:T(8,128)(2,1)} %get-tuple-element.36.q_ref.k_ref.v_ref), custom_call_target="tpu_custom_call" | custom-call | flops 8117488128 | bytes 9000000 | tf_op jit(solution)/shard_map/attn_forward/pallas_call | solution.py:177
  102.9 26.2 %all-gather.7.cloned.1.call-done.wo_ref = bf16[768,768]{1,0:T(8,128)(2,1)} async-done(((bf16[24,768]{1,0:T(8,128)(2,1)}), bf16[768,768]{1,0:T(8,128)(2,1)}) %all-gather.7.cloned.1.call-update) | async-done | bytes 1179664 | tf_op jit(solution)/shard_map/all_gather | solution.py:740
  129.1 65.4 %all-gather.9.cloned.1.call-done.wu_ref = bf16[768,3072]{1,0:T(8,128)(2,1)} async-done(((bf16[24,3072]{1,0:T(8,128)(2,1)}), bf16[768,3072]{1,0:T(8,128)(2,1)}) %all-gather.9.cloned.1.call-update) | async-done | bytes 4718608 | tf_op jit(solution)/shard_map/all_gather | solution.py:740
  194.5 18.5 %ffn_forward.1 = (f32[1024,768]{1,0:T(8,128)}, bf16[1024,768]{1,0:T(8,128)(2,1)}, bf16[1024,3072]{1,0:T(8,128)(2,1)}, bf16[1024,3072]{1,0:T(8,128)(2,1)}) custom-call(bf16[1024,768]{1,0:T(8,128)(2,1)} %get-tuple-element.37.ctx_ref, bf16[1024,768]{1,0:T(8,128)(2,1)} %x_ref.5, bf16[768,768]{1,0:T(8,128)(2,1)} %all-gather.7.cloned.1.call-done.wo_ref, ...), custom_call_target="tpu_custom_call" | custom-call | flops 6039797760 | bytes 28000000 | tf_op jit(solution)/shard_map/ffn_forward/pallas_call | solution.py:332
  213.0 46.7 %all-gather.11.cloned.1.call-done.wd_ref = bf16[3072,768]{1,0:T(8,128)(2,1)} async-done(((bf16[96,768]{1,0:T(8,128)(2,1)}), bf16[3072,768]{1,0:T(8,128)(2,1)}) %all-gather.11.cloned.1.call-update) | async-done | bytes 4718608 | tf_op jit(solution)/shard_map/all_gather | solution.py:740
  259.6 16.6 %up_grad.1 = (bf16[1024,3072]{1,0:T(8,128)(2,1)}, f32[1,3072]{1,0:T(1,128)}, bf16[16,24,3072]{2,1,0:T(8,128)(2,1)}, bf16[16,24,3072]{2,1,0:T(8,128)(2,1)}) custom-call(s32[33]{0:T(128)} %dynamic-slice_bitcast_fusion.table_ref, bf16[1024,768]{1,0:T(8,128)(2,1)} %dy_ref.5, bf16[3072,768]{1,0:T(8,128)(2,1)} %all-gather.11.cloned.1.call-done.wd_ref, ...), custom_call_target="tpu_custom_call" | custom-call | flops 9663676416 | bytes 25000000 | tf_op jit(solution)/shard_map/up_grad/pallas_call | solution.py:459
  276.2 19.2 %mid_back.1 = (f32[1024,768]{1,0:T(8,128)}, bf16[1024,768]{1,0:T(8,128)(2,1)}, f32[8,768]{1,0:T(8,128)}, bf16[16,24,768]{2,1,0:T(8,128)(2,1)}, bf16[16,24,768]{2,1,0:T(8,128)(2,1)}) custom-call(s32[33]{0:T(128)} %dynamic-slice_bitcast_fusion.table_ref, bf16[1024,3072]{1,0:T(8,128)(2,1)} %get-tuple-element.44.du_ref, ...), custom_call_target="tpu_custom_call" | custom-call | flops 7247757312 | bytes 26000000 | tf_op jit(solution)/shard_map/mid_back/pallas_call | solution.py:552
  295.7 27.8 %attn_backward.1 = (bf16[1024,768]{1,0:T(8,128)(2,1)}, bf16[1024,768]{1,0:T(8,128)(2,1)}, bf16[1024,384]{1,0:T(8,128)(2,1)}, f32[1024,384]{1,0:T(8,128)}) custom-call(s32[1,2]{1,0:T(1,128)} %bound_ref.3, bf16[1024,1536]{1,0:T(8,128)(2,1)} %get-tuple-element.41.qa_ref, bf16[1024,2304]{1,0:T(8,128)(2,1)} %get-tuple-element.36.q_ref.k_ref.v_ref, ...), custom_call_target="tpu_custom_call" | custom-call | flops 20293720064 | bytes 15000000 | tf_op jit(solution)/shard_map/attn_backward/pallas_call | solution.py:274
  323.5 9.6 %token_grad.1 = (f32[1024,768]{1,0:T(8,128)}, f32[8,768]{1,0:T(8,128)}) custom-call(bf16[1024,768]{1,0:T(8,128)(2,1)} %x_ref.5, bf16[1024,768]{1,0:T(8,128)(2,1)} %get-tuple-element.46.dq_ref, bf16[1024,768]{1,0:T(8,128)(2,1)} %get-tuple-element.47.dk_ref, bf16[1024,384]{1,0:T(8,128)(2,1)} %get-tuple-element.48.dv_ref, ...), custom_call_target="tpu_custom_call" | custom-call | flops 3019898880 | bytes 17000000 | tf_op jit(solution)/shard_map/token_grad/pallas_call | solution.py:616
  333.1 9.8 %in_grad.1 = (bf16[16,24,2048]{2,1,0:T(8,128)(2,1)}, bf16[16,24,2048]{2,1,0:T(8,128)(2,1)}) custom-call(s32[33]{0:T(128)} %dynamic-slice_bitcast_fusion.table_ref, bf16[1024,768]{1,0:T(8,128)(2,1)} %get-tuple-element.52.a1_ref, bf16[1024,768]{1,0:T(8,128)(2,1)} %get-tuple-element.46.dq_ref, bf16[1024,768]{1,0:T(8,128)(2,1)} %get-tuple-element.47.dk_ref, ...), custom_call_target="tpu_custom_call" | custom-call | flops 3019898880 | bytes 12000000 | tf_op jit(solution)/shard_map/in_grad/pallas_call | solution.py:675
  343.2 12.0 %down_grad.1 = (bf16[16,96,768]{2,1,0:T(8,128)(2,1)}, bf16[16,96,768]{2,1,0:T(8,128)(2,1)}) custom-call(s32[33]{0:T(128)} %dynamic-slice_bitcast_fusion.table_ref, bf16[1024,3072]{1,0:T(8,128)(2,1)} %get-tuple-element.39.act_ref, bf16[1024,768]{1,0:T(8,128)(2,1)} %dy_ref.5), custom_call_target="tpu_custom_call" | custom-call | flops 4831838208 | bytes 13000000 | tf_op jit(solution)/shard_map/down_grad/pallas_call | solution.py:420
  357.2 5.2 %collective-permute-done.6 = bf16[8,24,768]{2,1,0:T(8,128)(2,1)S(1)} collective-permute-done((bf16[8,24,768]{2,1,0:T(8,128)(2,1)S(1)}, bf16[8,24,768]{2,1,0:T(8,128)(2,1)S(1)}, u32[]{:S(2)}, u32[]{:S(2)}) %collective-permute-start.6) | collective-permute-done | bytes 294944 | tf_op jit(solution)/shard_map/ppermute | solution.py:715
  364.1 3.7 collective-permute-done.7
  372.3 10.3 %out_forward.1 = f32[1024,768]{1,0:T(8,128)} custom-call(bf16[1024,3072]{1,0:T(8,128)(2,1)} %get-tuple-element.39.act_ref, f32[1024,768]{1,0:T(8,128)} %get-tuple-element.40.mid_ref, bf16[3072,768]{1,0:T(8,128)(2,1)} %all-gather.11.cloned.1.call-done.wd_ref, f32[16,768]{1,0:T(8,128)} %get-tuple-element.38.vec_ref), custom_call_target="tpu_custom_call" | custom-call | flops 4831838208 | bytes 18000000 | tf_op jit(solution)/shard_map/out_forward/pallas_call | solution.py:359
  386.5 2.5 add_convert_fusion.1
  389.8 7.3 %collective-permute-done.2 = bf16[4,24,2048]{2,1,0:T(8,128)(2,1)S(1)} collective-permute-done((bf16[4,24,2048]{2,1,0:T(8,128)(2,1)S(1)}, bf16[4,24,2048]{2,1,0:T(8,128)(2,1)S(1)}, u32[]{:S(2)}, u32[]{:S(2)}) %collective-permute-start.2) | collective-permute-done | bytes 393248 | tf_op jit(solution)/shard_map/ppermute | solution.py:715
  400.1 5.9 %collective-permute-done.3 = bf16[2,24,2048]{2,1,0:T(8,128)(2,1)S(1)} collective-permute-done((bf16[2,24,2048]{2,1,0:T(8,128)(2,1)S(1)}, bf16[2,24,2048]{2,1,0:T(8,128)(2,1)S(1)}, u32[]{:S(2)}, u32[]{:S(2)}) %collective-permute-start.3) | collective-permute-done | bytes 196640 | tf_op jit(solution)/shard_map/ppermute | solution.py:715
  408.4 12.7 %collective-permute-done.11 = bf16[8,24,3072]{2,1,0:T(8,128)(2,1)S(1)} collective-permute-done((bf16[8,24,3072]{2,1,0:T(8,128)(2,1)S(1)}, bf16[8,24,3072]{2,1,0:T(8,128)(2,1)S(1)}, u32[]{:S(2)}, u32[]{:S(2)}) %collective-permute-start.11) | collective-permute-done | bytes 1179680 | tf_op jit(solution)/shard_map/ppermute | solution.py:715
  426.5 5.3 %collective-permute-done.12 = bf16[4,24,3072]{2,1,0:T(8,128)(2,1)S(1)} collective-permute-done((bf16[4,24,3072]{2,1,0:T(8,128)(2,1)S(1)}, bf16[4,24,3072]{2,1,0:T(8,128)(2,1)S(1)}, u32[]{:S(2)}, u32[]{:S(2)}) %collective-permute-start.12) | collective-permute-done | bytes 589856 | tf_op jit(solution)/shard_map/ppermute | solution.py:715
  435.7 7.2 %collective-permute-done.18 = bf16[2,96,768]{2,1,0:T(8,128)(2,1)S(1)} collective-permute-done((bf16[2,96,768]{2,1,0:T(8,128)(2,1)S(1)}, bf16[2,96,768]{2,1,0:T(8,128)(2,1)S(1)}, u32[]{:S(2)}, u32[]{:S(2)}) %collective-permute-start.18) | collective-permute-done | bytes 294944 | tf_op jit(solution)/shard_map/ppermute | solution.py:715
  443.1 4.7 %collective-permute-done.13 = bf16[2,24,3072]{2,1,0:T(8,128)(2,1)S(1)} collective-permute-done((bf16[2,24,3072]{2,1,0:T(8,128)(2,1)S(1)}, bf16[2,24,3072]{2,1,0:T(8,128)(2,1)S(1)}, u32[]{:S(2)}, u32[]{:S(2)}) %collective-permute-start.13) | collective-permute-done | bytes 294944 | tf_op jit(solution)/shard_map/ppermute | solution.py:715
  450.2 2.9 collective-permute-done.14
  (88 shorter events, 36.6 us)
Async XLA Ops:
  7.2 66.1 %all-gather.5.cloned.1.call-start = ((), (), s32[]{:S(2)}) async-start(), calls=%async_computation | async-start | bytes 3244032 | tf_op jit(solution)/shard_map/all_gather | solution.py:740
  9.6 119.5 %all-gather.7.cloned.1.call-start = ((), (), s32[]{:S(2)}) async-start(), calls=%async_computation.1 | async-start | bytes 1216512 | tf_op jit(solution)/shard_map/all_gather | solution.py:740
  10.3 184.2 %all-gather.9.cloned.1.call-start = ((), (), s32[]{:S(2)}) async-start(), calls=%async_computation.2 | async-start | bytes 4866048 | tf_op jit(solution)/shard_map/all_gather | solution.py:740
  11.0 248.6 %all-gather.11.cloned.1.call-start = ((), (), s32[]{:S(2)}) async-start(), calls=%async_computation.3 | async-start | bytes 4866048 | tf_op jit(solution)/shard_map/all_gather | solution.py:740
  295.4 60.1 %collective-permute-start.5 = (bf16[16,24,768]{2,1,0:T(8,128)(2,1)}, bf16[16,24,768]{2,1,0:T(8,128)(2,1)S(1)}, u32[]{:S(2)}, u32[]{:S(2)}) collective-permute-start(bf16[16,24,768]{2,1,0:T(8,128)(2,1)} %get-tuple-element.59), channel_id=1, source_target_pairs={{0,4},{1,5},{2,6},{3,7},{4,0},{5,1},{6,2},{7,3},{8,12},{9,13},{10,... | collective-permute-start | bytes 1769480 | tf_op jit(solution)/shard_map/ppermute | solution.py:715
  342.9 27.1 %collective-permute-start = (bf16[16,24,2048]{2,1,0:T(8,128)(2,1)}, bf16[16,24,2048]{2,1,0:T(8,128)(2,1)S(1)}, u32[]{:S(2)}, u32[]{:S(2)}) collective-permute-start(bf16[16,24,2048]{2,1,0:T(8,128)(2,1)} %get-tuple-element.57), channel_id=1, source_target_pairs={{0,4},{1,5},{2,6},{3,7},{4,0},{5,1},{6,2},{7,3},{8,12},{9,13},{10,... | collective-permute-start | bytes 4718600 | tf_op jit(solution)/shard_map/ppermute | solution.py:715
  355.3 28.1 %collective-permute-start.15 = (bf16[16,96,768]{2,1,0:T(8,128)(2,1)}, bf16[16,96,768]{2,1,0:T(8,128)(2,1)S(1)}, u32[]{:S(2)}, u32[]{:S(2)}) collective-permute-start(bf16[16,96,768]{2,1,0:T(8,128)(2,1)} %get-tuple-element.63), channel_id=1, source_target_pairs={{0,4},{1,5},{2,6},{3,7},{4,0},{5,1},{6,2},{7,3},{8,12},{9,13},{10,... | collective-permute-start | bytes 7077896 | tf_op jit(solution)/shard_map/ppermute | solution.py:715
  355.7 6.8 %collective-permute-start.6 = (bf16[8,24,768]{2,1,0:T(8,128)(2,1)S(1)}, bf16[8,24,768]{2,1,0:T(8,128)(2,1)S(1)}, u32[]{:S(2)}, u32[]{:S(2)}) collective-permute-start(bf16[8,24,768]{2,1,0:T(8,128)(2,1)S(1)} %slice.178), channel_id=1, source_target_pairs={{0,2},{1,3},{2,0},{3,1},{4,5},{5,4},{6,7},{7,6},{8,10},{9,11},{10,... | collective-permute-start | bytes 884744 | tf_op jit(solution)/shard_map/ppermute | solution.py:715
  362.6 5.2 %collective-permute-start.7 = (bf16[4,24,768]{2,1,0:T(8,128)(2,1)S(1)}, bf16[4,24,768]{2,1,0:T(8,128)(2,1)S(1)}, u32[]{:S(2)}, u32[]{:S(2)}) collective-permute-start(bf16[4,24,768]{2,1,0:T(8,128)(2,1)S(1)} %slice.180), channel_id=1, source_target_pairs={{0,1},{1,0},{2,3},{3,2},{4,6},{5,7},{6,4},{7,5},{8,9},{9,8},{10,11... | collective-permute-start | bytes 442376 | tf_op jit(solution)/shard_map/ppermute | solution.py:715
  364.1 22.5 %collective-permute-start.10 = (bf16[16,24,3072]{2,1,0:T(8,128)(2,1)}, bf16[16,24,3072]{2,1,0:T(8,128)(2,1)}, u32[]{:S(2)}, u32[]{:S(2)}) collective-permute-start(bf16[16,24,3072]{2,1,0:T(8,128)(2,1)} %get-tuple-element.61), channel_id=1, source_target_pairs={{0,4},{1,5},{2,6},{3,7},{4,0},{5,1},{6,2},{7,3},{8,12},{9,13},{10,... | collective-permute-start | bytes 7077896 | tf_op jit(solution)/shard_map/ppermute | solution.py:715
  367.8 14.8 %collective-permute-start.8 = (bf16[2,24,768]{2,1,0:T(8,128)(2,1)S(1)}, bf16[2,24,768]{2,1,0:T(8,128)(2,1)S(1)}, u32[]{:S(2)}, u32[]{:S(2)}) collective-permute-start(bf16[2,24,768]{2,1,0:T(8,128)(2,1)S(1)} %slice.182), channel_id=1, source_target_pairs={{0,16},{1,17},{2,18},{3,19},{4,20},{5,21},{6,22},{7,23},{8,24},{9,... | collective-permute-start | bytes 221192 | tf_op jit(solution)/shard_map/ppermute | solution.py:715
  370.8 14.0 %collective-permute-start.1 = (bf16[8,24,2048]{2,1,0:T(8,128)(2,1)S(1)}, bf16[8,24,2048]{2,1,0:T(8,128)(2,1)S(1)}, u32[]{:S(2)}, u32[]{:S(2)}) collective-permute-start(bf16[8,24,2048]{2,1,0:T(8,128)(2,1)S(1)} %slice.169), channel_id=1, source_target_pairs={{0,2},{1,3},{2,0},{3,1},{4,5},{5,4},{6,7},{7,6},{8,10},{9,11},{10,... | collective-permute-start | bytes 2359304 | tf_op jit(solution)/shard_map/ppermute | solution.py:715
  382.7 16.8 %collective-permute-start.9 = (bf16[1,24,768]{2,1,0:T(8,128)(2,1)S(1)}, bf16[1,24,768]{2,1,0:T(8,128)(2,1)S(1)}, u32[]{:S(2)}, u32[]{:S(2)}) collective-permute-start(bf16[1,24,768]{2,1,0:T(8,128)(2,1)S(1)} %slice.184), channel_id=1, source_target_pairs={{0,8},{1,9},{2,10},{3,11},{4,12},{5,13},{6,14},{7,15},{8,0},{9,1},... | collective-permute-start | bytes 110600 | tf_op jit(solution)/shard_map/ppermute | solution.py:715
  384.1 22.1 %collective-permute-start.16 = (bf16[8,96,768]{2,1,0:T(8,128)(2,1)S(1)}, bf16[8,96,768]{2,1,0:T(8,128)(2,1)S(1)}, u32[]{:S(2)}, u32[]{:S(2)}) collective-permute-start(bf16[8,96,768]{2,1,0:T(8,128)(2,1)S(1)} %slice.194), channel_id=1, source_target_pairs={{0,2},{1,3},{2,0},{3,1},{4,5},{5,4},{6,7},{7,6},{8,10},{9,11},{10,... | collective-permute-start | bytes 3538952 | tf_op jit(solution)/shard_map/ppermute | solution.py:715
  385.0 12.1 %collective-permute-start.2 = (bf16[4,24,2048]{2,1,0:T(8,128)(2,1)S(1)}, bf16[4,24,2048]{2,1,0:T(8,128)(2,1)S(1)}, u32[]{:S(2)}, u32[]{:S(2)}) collective-permute-start(bf16[4,24,2048]{2,1,0:T(8,128)(2,1)S(1)} %slice.171), channel_id=1, source_target_pairs={{0,1},{1,0},{2,3},{3,2},{4,6},{5,7},{6,4},{7,5},{8,9},{9,8},{10,11... | collective-permute-start | bytes 1179656 | tf_op jit(solution)/shard_map/ppermute | solution.py:715
  389.2 31.9 %collective-permute-start.11 = (bf16[8,24,3072]{2,1,0:T(8,128)(2,1)S(1)}, bf16[8,24,3072]{2,1,0:T(8,128)(2,1)S(1)}, u32[]{:S(2)}, u32[]{:S(2)}) collective-permute-start(bf16[8,24,3072]{2,1,0:T(8,128)(2,1)S(1)} %slice.186), channel_id=1, source_target_pairs={{0,2},{1,3},{2,0},{3,1},{4,5},{5,4},{6,7},{7,6},{8,10},{9,11},{10,... | collective-permute-start | bytes 3538952 | tf_op jit(solution)/shard_map/ppermute | solution.py:715
  397.3 8.7 %collective-permute-start.3 = (bf16[2,24,2048]{2,1,0:T(8,128)(2,1)S(1)}, bf16[2,24,2048]{2,1,0:T(8,128)(2,1)S(1)}, u32[]{:S(2)}, u32[]{:S(2)}) collective-permute-start(bf16[2,24,2048]{2,1,0:T(8,128)(2,1)S(1)} %slice.173), channel_id=1, source_target_pairs={{0,16},{1,17},{2,18},{3,19},{4,20},{5,21},{6,22},{7,23},{8,24},{9,... | collective-permute-start | bytes 589832 | tf_op jit(solution)/shard_map/ppermute | solution.py:715
  406.1 17.9 %collective-permute-start.4 = (bf16[1,24,2048]{2,1,0:T(8,128)(2,1)S(1)}, bf16[1,24,2048]{2,1,0:T(8,128)(2,1)S(1)}, u32[]{:S(2)}, u32[]{:S(2)}) collective-permute-start(bf16[1,24,2048]{2,1,0:T(8,128)(2,1)S(1)} %slice.175), channel_id=1, source_target_pairs={{0,8},{1,9},{2,10},{3,11},{4,12},{5,13},{6,14},{7,15},{8,0},{9,1},... | collective-permute-start | bytes 294920 | tf_op jit(solution)/shard_map/ppermute | solution.py:715
  406.5 17.5 %collective-permute-start.17 = (bf16[4,96,768]{2,1,0:T(8,128)(2,1)S(1)}, bf16[4,96,768]{2,1,0:T(8,128)(2,1)S(1)}, u32[]{:S(2)}, u32[]{:S(2)}) collective-permute-start(bf16[4,96,768]{2,1,0:T(8,128)(2,1)S(1)} %slice.196), channel_id=1, source_target_pairs={{0,1},{1,0},{2,3},{3,2},{4,6},{5,7},{6,4},{7,5},{8,9},{9,8},{10,11... | collective-permute-start | bytes 1769480 | tf_op jit(solution)/shard_map/ppermute | solution.py:715
  421.6 10.2 %collective-permute-start.12 = (bf16[4,24,3072]{2,1,0:T(8,128)(2,1)S(1)}, bf16[4,24,3072]{2,1,0:T(8,128)(2,1)S(1)}, u32[]{:S(2)}, u32[]{:S(2)}) collective-permute-start(bf16[4,24,3072]{2,1,0:T(8,128)(2,1)S(1)} %slice.188), channel_id=1, source_target_pairs={{0,1},{1,0},{2,3},{3,2},{4,6},{5,7},{6,4},{7,5},{8,9},{9,8},{10,11... | collective-permute-start | bytes 1769480 | tf_op jit(solution)/shard_map/ppermute | solution.py:715
  424.2 18.7 %collective-permute-start.18 = (bf16[2,96,768]{2,1,0:T(8,128)(2,1)S(1)}, bf16[2,96,768]{2,1,0:T(8,128)(2,1)S(1)}, u32[]{:S(2)}, u32[]{:S(2)}) collective-permute-start(bf16[2,96,768]{2,1,0:T(8,128)(2,1)S(1)} %slice.198), channel_id=1, source_target_pairs={{0,16},{1,17},{2,18},{3,19},{4,20},{5,21},{6,22},{7,23},{8,24},{9,... | collective-permute-start | bytes 884744 | tf_op jit(solution)/shard_map/ppermute | solution.py:715
  432.0 15.8 %collective-permute-start.13 = (bf16[2,24,3072]{2,1,0:T(8,128)(2,1)S(1)}, bf16[2,24,3072]{2,1,0:T(8,128)(2,1)S(1)}, u32[]{:S(2)}, u32[]{:S(2)}) collective-permute-start(bf16[2,24,3072]{2,1,0:T(8,128)(2,1)S(1)} %slice.190), channel_id=1, source_target_pairs={{0,16},{1,17},{2,18},{3,19},{4,20},{5,21},{6,22},{7,23},{8,24},{9,... | collective-permute-start | bytes 884744 | tf_op jit(solution)/shard_map/ppermute | solution.py:715
  443.0 6.5 %collective-permute-start.19 = (bf16[1,96,768]{2,1,0:T(8,128)(2,1)S(1)}, bf16[1,96,768]{2,1,0:T(8,128)(2,1)S(1)}, u32[]{:S(2)}, u32[]{:S(2)}) collective-permute-start(bf16[1,96,768]{2,1,0:T(8,128)(2,1)S(1)} %slice.200), channel_id=1, source_target_pairs={{0,8},{1,9},{2,10},{3,11},{4,12},{5,13},{6,14},{7,15},{8,0},{9,1},... | collective-permute-start | bytes 442376 | tf_op jit(solution)/shard_map/ppermute | solution.py:715
  447.9 5.2 %collective-permute-start.14 = (bf16[1,24,3072]{2,1,0:T(8,128)(2,1)S(1)}, bf16[1,24,3072]{2,1,0:T(8,128)(2,1)S(1)}, u32[]{:S(2)}, u32[]{:S(2)}) collective-permute-start(bf16[1,24,3072]{2,1,0:T(8,128)(2,1)S(1)} %slice.192), channel_id=1, source_target_pairs={{0,8},{1,9},{2,10},{3,11},{4,12},{5,13},{6,14},{7,15},{8,0},{9,1},... | collective-permute-start | bytes 442376 | tf_op jit(solution)/shard_map/ppermute | solution.py:715
  (4 other events, 40.1 us)
Sparse Core Ops, SparseCore 0:
  11.5 61.7 all-gather.4
  76.1 52.8 all-gather.6
  132.0 62.4 all-gather.8
  197.2 62.3 all-gather.10
